TPU v7x, 32 devices: a whole 2x2x4 slice. The times are simulated.
32 devices in a mesh: groups: 2 (over y), tile: 4 (over z), rep: 2 (over x), sub: 2 (over core).
Axes of the slice: x: 2, y: 2, z: 4, core: 2. Of those that a mesh axis runs over, the one named last changes fastest.
Arguments:
- amplitudes: bfloat16 [4096, 2048], P(('groups', 'tile', 'sub'), 'rep'), parts along dimension 0, may hold values from -6 to 6
- amp_mask: int32 [32, 16], P(('groups', 'tile', 'sub'), 'rep'), parts along dimension 0, may hold values 0 or 1
- integrals: bfloat16 [2048, 4096], P('rep', 'tile'), may hold values from -0.125 to 0.125
- int_mask: int32 [16, 32], P('rep', 'tile'), may hold values 0 or 1
- owner_map: int32 [8], P('groups'), parts along dimension 0, may hold values from 0 to 3
Outputs:
- ladder: bfloat16 [8, 512, 4096], P('groups', 'sub', ('tile', 'rep')), parts along dimension 0
There are 2 independent parts, one for each index of `groups`. A program takes and returns all parts, laid end to end along the dimension named above; an argument that names none is the same for every part. Nothing has to cross between parts.
Inputs may be any that keep to these rules, and one draw needn't show every extreme that they name: `owner_map`: block owners, any of them, repeats allowed.
All inputs are finite; a program needn't handle non-finite values. No bound on the sum of `amp_mask` or of `int_mask` on one device may be relied on, other than what follows from the above.
Results may differ from a plain program's by a relative error of at most 0.0052.
Values may be sent and summed in bfloat16 or wider, within the bound.
A program may use at most 64 MiB of HBM per device.

v0:
```python
import jax
import jax.numpy as jnp
from jax import lax
from jax.sharding import PartitionSpec as P

TILE = 128
STEPS = 4


def from_root(block, axis, source):
    block = jnp.where(lax.axis_index(axis) == source, block, jnp.zeros_like(block))
    return lax.psum(block, axis)


def expand_mask(mask):
    big = jnp.repeat(jnp.repeat(mask, TILE, axis=0), TILE, axis=1)
    return big.astype(jnp.bfloat16)


def shards(amplitudes, amp_mask, integrals, int_mask, owner_map):
    masked_amp = amplitudes * expand_mask(amp_mask)
    masked_int = integrals * expand_mask(int_mask)
    results = []
    for step in range(STEPS):
        block_rows = from_root(masked_amp, "tile", owner_map[step])
        partial_value = jnp.dot(block_rows, masked_int, preferred_element_type=jnp.float32)
        summed = lax.psum_scatter(
            partial_value.astype(jnp.bfloat16), "rep", scatter_dimension=1, tiled=True
        )
        results.append(summed)
    return jnp.stack(results, axis=0)


def solution(mesh):
    placed = (
        P(("groups", "tile", "sub"), "rep"),
        P(("groups", "tile", "sub"), "rep"),
        P("rep", "tile"),
        P("rep", "tile"),
        P("groups"),
    )
    return jax.shard_map(
        shards,
        mesh=mesh,
        in_specs=placed,
        out_specs=P("groups", "sub", ("tile", "rep")),
        check_vma=False,
    )
```

profile of v0, /device:TPU:0, one launch (start us, length us, event | category | flops | bytes accessed | tf_op | source)
XLA Modules:
  0.0 181.7 jit_solution(7761216337371380628)
XLA Ops:
  6.5 0.0 all-reduce.3.cloned.1.call-start
  6.5 0.7 convert_element_type.34
  7.2 1.4 fusion
  11.1 0.3 broadcast_in_dim.13
  11.5 1.9 %broadcast_select_fusion.3 = (bf16[256,1024]{1,0:T(8,128)(2,1)}, bf16[256,1024]{1,0:T(8,128)(2,1)S(1)}) fusion(pred[]{:T(512)S(6)} %eq.12, bf16[256,1024]{1,0:T(8,128)(2,1)} %param.5, bf16[32,8,8,128]{3,2,1,0:T(8,128)(2,1)S(1)} %bitcast.26), kind=kLoop, calls=%fused_computation.10 | loop fusion | flops 524288 | bytes 2097153 | tf_op jit(solution)/shard_map/jit(_where)/select_n | solution.py:11
  13.4 1.2 broadcast_select_fusion.2
  14.6 0.0 all-reduce.3.cloned.1.call-update
  14.6 0.0 reduce-scatter.5.cloned.1.call-start
  14.7 0.0 copy-done.2
  14.8 2.9 %broadcast_in_dim.15 = bf16[1024,8,128]{2,1,0:T(8,128)(2,1)S(1)} broadcast(bf16[1024,8]{1,0:T(8,128)(2,1)S(1)} %bitcast.27), dimensions={0,1} | broadcast | bytes 2113536 | tf_op jit(solution)/shard_map/broadcast_in_dim | solution.py:16
  17.7 0.0 copy-done
  17.7 1.6 bitcast_multiply_fusion
  19.3 86.2 %all-reduce.3.cloned.1.call-done = (bf16[256,1024]{1,0:T(8,128)(2,1)}, bf16[256,1024]{1,0:T(8,128)(2,1)}, bf16[256,1024]{1,0:T(8,128)(2,1)}, bf16[256,1024]{1,0:T(8,128)(2,1)}) async-done(((bf16[256,1024]{1,0:T(8,128)(2,1)}, bf16[256,1024]{1,0:T(8,128)(2,1)}, bf16[256,1024]{1,0:T(8,128)(2,1)}, bf16[256,1024]{1,0:T(8,128)(2,1)}), (bf16[256,1024]{1,0:T(8,128)(2,1)}, bf16[256,1024]{1,0:T(8,128)(2,1)}, ...) | async-done | bytes 2097168 | tf_op jit(solution)/shard_map/psum | solution.py:12
  105.5 3.3 %convolution_convert_fusion.3 = bf16[256,1024]{1,0:T(8,128)(2,1)} fusion(bf16[256,1024]{1,0:T(8,128)(2,1)} %get-tuple-element.8, bf16[1024,1024]{1,0:T(8,128)(2,1)} %bitcast_multiply_fusion), kind=kOutput, calls=%fused_computation.4 | convolution fusion | flops 537133056 | bytes 3145728 | tf_op jit(solution)/shard_map/dot_general | solution.py:26
  108.9 0.0 reduce-scatter.5.cloned.1.call-update
  108.9 0.0 copy-start.4
  108.9 0.0 reduce-scatter.7.cloned.1.call-start
  109.0 0.0 copy-done.1
  109.0 0.0 copy-done.5
  109.0 1.5 convolution_convert_fusion.2
  110.5 0.0 reduce-scatter.7.cloned.1.call-update
  110.5 0.0 reduce-scatter.9.cloned.1.call-start
  110.6 1.5 convolution_convert_fusion.1
  112.1 0.0 reduce-scatter.9.cloned.1.call-update
  112.1 0.0 reduce-scatter.11.cloned.1.call-start
  112.2 1.5 convolution_convert_fusion
  113.7 0.0 reduce-scatter.11.cloned.1.call-update
  113.7 8.8 %reduce-scatter.5.cloned.1.call-done = bf16[256,512]{1,0:T(8,128)(2,1)} async-done(((bf16[256,1024]{1,0:T(8,128)(2,1)}), bf16[256,512]{1,0:T(8,128)(2,1)}) %reduce-scatter.5.cloned.1.call-update) | async-done | bytes 262160 | tf_op jit(solution)/shard_map/reduce_scatter | solution.py:27
  122.5 16.8 %reduce-scatter.7.cloned.1.call-done = bf16[256,512]{1,0:T(8,128)(2,1)} async-done(((bf16[256,1024]{1,0:T(8,128)(2,1)}), bf16[256,512]{1,0:T(8,128)(2,1)}) %reduce-scatter.7.cloned.1.call-update) | async-done | bytes 262160 | tf_op jit(solution)/shard_map/reduce_scatter | solution.py:27
  139.4 16.8 %reduce-scatter.9.cloned.1.call-done = bf16[256,512]{1,0:T(8,128)(2,1)} async-done(((bf16[256,1024]{1,0:T(8,128)(2,1)}), bf16[256,512]{1,0:T(8,128)(2,1)}) %reduce-scatter.9.cloned.1.call-update) | async-done | bytes 262160 | tf_op jit(solution)/shard_map/reduce_scatter | solution.py:27
  156.2 16.7 %reduce-scatter.11.cloned.1.call-done = bf16[256,512]{1,0:T(8,128)(2,1)} async-done(((bf16[256,1024]{1,0:T(8,128)(2,1)}), bf16[256,512]{1,0:T(8,128)(2,1)}) %reduce-scatter.11.cloned.1.call-update) | async-done | bytes 262160 | tf_op jit(solution)/shard_map/reduce_scatter | solution.py:27
  172.8 2.3 %pad_maximum_fusion = bf16[4,256,512]{2,1,0:T(8,128)(2,1)} fusion(bf16[1,256,512]{2,1,0:T(8,128)(2,1)} %bitcast.32, bf16[1,256,512]{2,1,0:T(8,128)(2,1)} %bitcast.31, bf16[1,256,512]{2,1,0:T(8,128)(2,1)} %bitcast.30, bf16[1,256,512]{2,1,0:T(8,128)(2,1)} %bitcast.29), kind=kLoop, calls=%fused_computation.5 | loop fusion | flops 1572864 | bytes 2097152 | tf_op jit(solution)/shard_map/stack | solution.py:31
  (10 shorter events, 0.1 us)
Async XLA Ops:
  6.5 99.0 %all-reduce.3.cloned.1.call-start = ((), (), s32[]{:S(2)}) async-start(), calls=%async_computation.8 | async-start | bytes 4194304 | tf_op jit(solution)/shard_map/psum | solution.py:12
  13.4 1.3 copy-start.2
  14.6 3.1 %copy-start = (bf16[1024,1024]{1,0:T(8,128)(2,1)S(1)}, bf16[1024,1024]{1,0:T(8,128)(2,1)}, u32[]{:S(2)}) copy-start(bf16[1024,1024]{1,0:T(8,128)(2,1)} %param.7) | copy-start | bytes 6291460
  14.6 107.9 %reduce-scatter.5.cloned.1.call-start = ((), (), s32[]{:S(2)}) async-start(), calls=%async_computation.4 | async-start | bytes 786432 | tf_op jit(solution)/shard_map/reduce_scatter | solution.py:27
  19.3 89.6 %copy-start.1 = (bf16[1024,1024]{1,0:T(8,128)(2,1)S(1)}, bf16[1024,1024]{1,0:T(8,128)(2,1)}, u32[]{:S(2)}) copy-start(bf16[1024,1024]{1,0:T(8,128)(2,1)} %bitcast_multiply_fusion) | copy-start | bytes 6291460
  105.5 3.4 %copy-start.5 = (bf16[256,1024]{1,0:T(8,128)(2,1)S(1)}, bf16[256,1024]{1,0:T(8,128)(2,1)}, u32[]{:S(2)}) copy-start(bf16[256,1024]{1,0:T(8,128)(2,1)} %get-tuple-element.7) | copy-start | bytes 1572868
  108.9 1.7 copy-start.4
  108.9 30.5 %reduce-scatter.7.cloned.1.call-start = ((), (), s32[]{:S(2)}) async-start(), calls=%async_computation.5 | async-start | bytes 786432 | tf_op jit(solution)/shard_map/reduce_scatter | solution.py:27
  110.5 1.7 copy-start.3
  110.5 45.6 %reduce-scatter.9.cloned.1.call-start = ((), (), s32[]{:S(2)}) async-start(), calls=%async_computation.6 | async-start | bytes 786432 | tf_op jit(solution)/shard_map/reduce_scatter | solution.py:27
  112.1 60.7 %reduce-scatter.11.cloned.1.call-start = ((), (), s32[]{:S(2)}) async-start(), calls=%async_computation.7 | async-start | bytes 786432 | tf_op jit(solution)/shard_map/reduce_scatter | solution.py:27
Sparse Core Ops, SparseCore 0:
  14.8 90.7 all-reduce.2
  109.0 13.4 reduce-scatter.4
  124.8 14.5 reduce-scatter.6
  141.6 14.5 reduce-scatter.8
  158.2 14.5 reduce-scatter.10
where the time goes:
time: 182 us
  waiting for transfers between devices  145 us (80%)
  between operations  15.7 us (9%)
  matrix products  7.87 us (4%)
  other arithmetic  7.72 us (4%)
  local copies, waits for them, and re-layouts  4.76 us (3%)
    psum x1, waiting for transfers between devices, from_root(): return lax.psum(block, axis)  86.2 us
    reduce_scatter x4, waiting for transfers between devices, shards(): lax.psum_scatter(partial_value.astype(jnp.bfloat16), 'rep', scatter_dimen...  59.1 us
    dot_general x4, matrix products, shards(): jnp.dot(block_rows, masked_int, preferred_element_type=jnp.float32)  7.87 us
  transfers between devices with their start and end apart: 5, of which 5 were waited for; matrix products, arithmetic and copies ran while one was open for 5% of the time, Pallas kernels for 0%

commit v1 on v0

v1 whole, which is shorter than its diff:
```python
import functools

import jax
import jax.numpy as jnp
from jax import lax
from jax.experimental import pallas as pl
from jax.experimental.pallas import tpu as pltpu
from jax.sharding import PartitionSpec as P

TILE = 128
CHUNKS = 4
MESH = pl.DeviceIdType.MESH


def expand_mask(mask):
    big = jnp.repeat(jnp.repeat(mask, TILE, axis=0), TILE, axis=1)
    return big.astype(jnp.bfloat16)


def from_root(block, axis, source):
    block = jnp.where(lax.axis_index(axis) == source, block, jnp.zeros_like(block))
    return lax.psum(block, axis)


def stepwise(amplitudes, amp_mask, integrals, int_mask, owner_map):
    masked_amp = amplitudes * expand_mask(amp_mask)
    masked_int = integrals * expand_mask(int_mask)
    results = []
    for step in range(owner_map.shape[0]):
        block_rows = from_root(masked_amp, "tile", owner_map[step])
        partial_value = jnp.dot(block_rows, masked_int, preferred_element_type=jnp.float32)
        summed = lax.psum_scatter(
            partial_value.astype(jnp.bfloat16), "rep", scatter_dimension=1, tiled=True
        )
        results.append(summed)
    return jnp.stack(results, axis=0)


def tile_scale(mask_ref, i, j, shape):
    return jnp.full(shape, mask_ref[i, j].astype(jnp.float32), jnp.float32).astype(jnp.bfloat16)


def gather_kernel(
    n, reps, amp_mask, int_mask, amp_hbm, int_hbm, out_ref,
    blocks, ints, mine, sent, got,
    load_sem, up_send, up_recv, down_send, down_recv, x_send, x_recv,
):
    z = lax.axis_index("tile")
    x = lax.axis_index("rep")
    rows, depth = amp_hbm.shape
    part = rows // CHUNKS
    width = int_hbm.shape[1] // reps

    load_amp = pltpu.make_async_copy(amp_hbm, blocks.at[z], load_sem.at[0])
    load_int = pltpu.make_async_copy(int_hbm, ints, load_sem.at[1])
    load_amp.start()
    load_int.start()

    barrier = pltpu.get_barrier_semaphore()

    @pl.when(z > 0)
    def _():
        pl.semaphore_signal(barrier, inc=1, device_id={"tile": z - 1}, device_id_type=MESH)

    @pl.when(z < n - 1)
    def _():
        pl.semaphore_signal(barrier, inc=1, device_id={"tile": z + 1}, device_id_type=MESH)

    for k in range(1, reps):
        pl.semaphore_signal(barrier, inc=1, device_id={"rep": lax.rem(x + k, reps)}, device_id_type=MESH)
    pl.semaphore_wait(barrier, jnp.where(z > 0, 1, 0) + jnp.where(z < n - 1, 1, 0) + (reps - 1))

    def span(c):
        return pl.ds(pl.multiple_of(c * part, part), part)

    def up(b, c):
        piece = blocks.at[b, span(c)]
        return pltpu.make_async_remote_copy(
            src_ref=piece, dst_ref=piece, send_sem=up_send.at[b, c], recv_sem=up_recv.at[b, c],
            device_id={"tile": z + 1}, device_id_type=MESH)

    def down(b, c):
        piece = blocks.at[b, span(c)]
        return pltpu.make_async_remote_copy(
            src_ref=piece, dst_ref=piece, send_sem=down_send.at[b, c], recv_sem=down_recv.at[b, c],
            device_id={"tile": z - 1}, device_id_type=MESH)

    def across(k, b, c):
        return pltpu.make_async_remote_copy(
            src_ref=sent.at[k - 1, b, span(c)], dst_ref=got.at[k - 1, b, span(c)],
            send_sem=x_send.at[k - 1, b, c], recv_sem=x_recv.at[k - 1, b, c],
            device_id={"rep": lax.rem(x + k, reps)}, device_id_type=MESH)

    def columns(r):
        return pl.ds(pl.multiple_of(r * width, width), width)

    def compute(b, c):
        for k in range(1, reps):
            sent[k - 1, b, span(c), :] = jnp.dot(
                blocks[b, span(c), :], ints[:, columns(lax.rem(x + k, reps))],
                preferred_element_type=jnp.float32).astype(jnp.bfloat16)
            across(k, b, c).start()
        mine[b, span(c), :] = jnp.dot(
            blocks[b, span(c), :], ints[:, columns(x)],
            preferred_element_type=jnp.float32).astype(jnp.bfloat16)

    def finish(b, c):
        total = mine[b, span(c), :].astype(jnp.float32)
        for k in range(1, reps):
            across(k, b, c).wait_recv()
            total = total + got[k - 1, b, span(c), :].astype(jnp.float32)
        out_ref[b, span(c), :] = total.astype(jnp.bfloat16)

    load_amp.wait()
    for c in range(CHUNKS):
        at = slice(c * part, (c + 1) * part)
        for j in range(depth // TILE):
            here = slice(j * TILE, (j + 1) * TILE)
            scale = tile_scale(amp_mask, c * part // TILE, j, (part, TILE))
            blocks[z, at, here] = blocks[z, at, here] * scale

        @pl.when(z < n - 1)
        def _():
            up(z, c).start()

        @pl.when(z > 0)
        def _():
            down(z, c).start()

    load_int.wait()
    for j in range(int_hbm.shape[1] // TILE):
        here = slice(j * TILE, (j + 1) * TILE)

        @pl.loop(0, depth // TILE)
        def _(i):
            at = pl.ds(pl.multiple_of(i * TILE, TILE), TILE)
            ints[at, here] = ints[at, here] * tile_scale(int_mask, i, j, (TILE, TILE))

    @pl.loop(0, CHUNKS)
    def _(c):
        compute(z, c)

    @pl.loop(1, n)
    def _(d):
        lower, upper = z - d, z + d

        @pl.loop(0, CHUNKS)
        def _(c):
            @pl.when(lower >= 0)
            def _():
                up(lower, c).wait_recv()

                @pl.when(z < n - 1)
                def _():
                    up(lower, c).start()

            @pl.when(upper < n)
            def _():
                down(upper, c).wait_recv()

                @pl.when(z > 0)
                def _():
                    down(upper, c).start()

            @pl.when(lower >= 0)
            def _():
                compute(lower, c)

            @pl.when(upper < n)
            def _():
                compute(upper, c)

            @pl.when(lower + 1 >= 0)
            def _():
                finish(lower + 1, c)

            @pl.when((upper - 1 < n) & (d > 1))
            def _():
                finish(upper - 1, c)

    @pl.loop(0, CHUNKS)
    def _(c):
        @pl.when(z == n - 1)
        def _():
            finish(0, c)

        @pl.when(z == 0)
        def _():
            finish(n - 1, c)

    @pl.loop(0, n)
    def _(b):
        @pl.loop(0, CHUNKS)
        def _(c):
            for k in range(1, reps):
                across(k, b, c).wait_send()

            @pl.when((b <= z) & (z < n - 1))
            def _():
                up(b, c).wait_send()

            @pl.when((b >= z) & (z > 0))
            def _():
                down(b, c).wait_send()


def pick_kernel(owner_ref, block_ref, out_ref):
    out_ref[...] = block_ref[...]


def gathered(n, reps, amplitudes, amp_mask, integrals, int_mask, owner_map):
    rows, depth = amplitudes.shape
    wide = integrals.shape[1]
    width = wide // reps
    steps = owner_map.shape[0]
    dma = pltpu.SemaphoreType.DMA
    bf16 = jnp.bfloat16
    by_owner = pl.pallas_call(
        functools.partial(gather_kernel, n, reps),
        out_shape=jax.ShapeDtypeStruct((n, rows, width), bf16),
        in_specs=[pl.BlockSpec(memory_space=pltpu.SMEM)] * 2 + [pl.BlockSpec(memory_space=pl.ANY)] * 2,
        out_specs=pl.BlockSpec(memory_space=pltpu.VMEM),
        scratch_shapes=[
            pltpu.VMEM((n, rows, depth), bf16),
            pltpu.VMEM((depth, wide), bf16),
            pltpu.VMEM((n, rows, width), bf16),
            pltpu.VMEM((reps - 1, n, rows, width), bf16),
            pltpu.VMEM((reps - 1, n, rows, width), bf16),
            dma((2,)),
            dma((n, CHUNKS)), dma((n, CHUNKS)), dma((n, CHUNKS)), dma((n, CHUNKS)),
            dma((reps - 1, n, CHUNKS)), dma((reps - 1, n, CHUNKS)),
        ],
        compiler_params=pltpu.CompilerParams(
            collective_id=0, has_side_effects=True, vmem_limit_bytes=40 * 1024 * 1024),
        cost_estimate=pl.CostEstimate(
            flops=2 * n * rows * depth * wide, bytes_accessed=2 * (rows * depth + depth * wide + n * rows * width),
            transcendentals=0),
    )(amp_mask, int_mask, amplitudes, integrals)
    return pl.pallas_call(
        pick_kernel,
        out_shape=jax.ShapeDtypeStruct((steps, rows, width), bf16),
        grid_spec=pltpu.PrefetchScalarGridSpec(
            num_scalar_prefetch=1,
            grid=(steps,),
            in_specs=[pl.BlockSpec((1, rows, width), lambda s, owner: (owner[s], 0, 0))],
            out_specs=pl.BlockSpec((1, rows, width), lambda s, owner: (s, 0, 0)),
        ),
    )(owner_map, by_owner)


def solution(mesh):
    n, reps = mesh.shape["tile"], mesh.shape["rep"]

    def shards(amplitudes, amp_mask, integrals, int_mask, owner_map):
        if n > owner_map.shape[0]:
            return stepwise(amplitudes, amp_mask, integrals, int_mask, owner_map)
        return gathered(n, reps, amplitudes, amp_mask, integrals, int_mask, owner_map)

    placed = (
        P(("groups", "tile", "sub"), "rep"),
        P(("groups", "tile", "sub"), "rep"),
        P("rep", "tile"),
        P("rep", "tile"),
        P("groups"),
    )
    return jax.shard_map(
        shards,
        mesh=mesh,
        in_specs=placed,
        out_specs=P("groups", "sub", ("tile", "rep")),
        check_vma=False,
    )
```

time: 182 us -> 54 us (0.30)
  waiting for transfers between devices: 145 us -> 0 us
  Pallas kernels: 0 us -> 48.7 us
  between operations: 15.7 us -> 0.02 us
  matrix products: 7.87 us -> 0 us
  other arithmetic: 7.72 us -> 0 us
    psum x1 -> x0, waiting for transfers between devices: 86.2 us -> none  [from_root(): return lax.psum(block, axis)]
    reduce_scatter x4 -> x0, waiting for transfers between devices: 59.1 us -> none  [shards(): lax.psum_scatter(partial_value.astype(jnp.bfloat16), 'rep', scatter_dimen...]
    pallas_call x0 -> x2, Pallas kernels: none -> 48.7 us  [the longest x1 44.6 us: gathered(): pl.pallas_call(functools.partial(gather_kernel, n, reps), out_shape=jax.S...]
    dot_general x4 -> x0, matrix products: 7.87 us -> none  [shards(): jnp.dot(block_rows, masked_int, preferred_element_type=jnp.float32)]
    unnamed x12 -> x10, local copies, waits for them, and re-layouts: 0.02 us -> 4.95 us
    broadcast_in_dim x4 -> x0, local copies, waits for them, and re-layouts: 3.32 us -> none  [expand_mask(): big = jnp.repeat(jnp.repeat(mask, TILE, axis=0), TILE, axis=1)]
    select_n x2 -> x0, other arithmetic: 3.14 us -> none  [from_root(): jnp.where(lax.axis_index(axis) == source, block, jnp.zeros_like(block))]
    another operation x1 -> x0, other arithmetic: 2.29 us -> none  [shards(): return jnp.stack(results, axis=0)]
  transfers between devices with their start and end apart: 5 -> 0, of which waited for: 5 -> 0; matrix products, arithmetic and copies ran while one was open for 5% -> 0% of each run, Pallas kernels for 0% -> 0%
where the time goes in v1:
time: 54 us; the launch traced here: 53.7 us
  Pallas kernels  48.7 us (90%)
  local copies, waits for them, and re-layouts  4.95 us (9%)
    pallas_call x1, Pallas kernels, gathered(): pl.pallas_call(functools.partial(gather_kernel, n, reps), out_shape=jax.S...  44.6 us
    unnamed x10, local copies, waits for them, and re-layouts  4.95 us
    pallas_call x1, Pallas kernels, gathered(): pl.pallas_call(pick_kernel, out_shape=jax.ShapeDtypeStruct((steps, rows,...  4.03 us

profile of v1, /device:TPU:0, one launch (start us, length us, event | category | flops | bytes accessed | tf_op | source)
XLA Modules:
  0.0 53.7 jit_solution(9859895761184257001)
XLA Ops:
  0.0 0.0 copy-start.1
  0.0 1.6 %copy-done.1 = bf16[1024,1024]{1,0:T(8,128)(2,1)S(1)} copy-done((bf16[1024,1024]{1,0:T(8,128)(2,1)S(1)}, bf16[1024,1024]{1,0:T(8,128)(2,1)}, u32[]{:S(2)}) %copy-start.1) | copy-done | bytes 2097176
  1.6 0.0 copy-start.2
  1.6 1.0 %copy-done.2 = bf16[256,1024]{1,0:T(8,128)(2,1)S(1)} copy-done((bf16[256,1024]{1,0:T(8,128)(2,1)S(1)}, bf16[256,1024]{1,0:T(8,128)(2,1)}, u32[]{:S(2)}) %copy-start.2) | copy-done | bytes 524312
  2.6 0.0 copy-start.3
  2.6 0.7 %copy-done.3 = s32[8,8]{1,0:T(8,128)S(1)} copy-done((s32[8,8]{1,0:T(8,128)S(1)}, s32[8,8]{1,0:T(8,128)}, u32[]{:S(2)}) %copy-start.3) | copy-done | bytes 280
  3.3 0.0 copy-start.4
  3.3 0.7 %copy-done.4 = s32[2,8]{1,0:T(2,128)S(1)} copy-done((s32[2,8]{1,0:T(2,128)S(1)}, s32[2,8]{1,0:T(2,128)}, u32[]{:S(2)}) %copy-start.4) | copy-done | bytes 88
  4.0 44.6 %shard_map.55.block_ref = bf16[4,256,512]{2,1,0:T(8,128)(2,1)S(1)} custom-call(s32[2,8]{1,0:T(2,128)S(1)} %copy-done.4, s32[8,8]{1,0:T(8,128)S(1)} %copy-done.3, bf16[256,1024]{1,0:T(8,128)(2,1)S(1)} %copy-done.2, bf16[1024,1024]{1,0:T(8,128)(2,1)S(1)} %copy-done.1), custom_call_target="tpu_custom_call" | custom-call | flops 2147483648 | bytes 3670016 | tf_op jit(solution)/shard_map/pallas_call | solution.py:218
  48.7 0.0 copy-start
  48.7 1.0 %copy-done = bf16[4,256,512]{2,1,0:T(8,128)(2,1)} copy-done((bf16[4,256,512]{2,1,0:T(8,128)(2,1)}, bf16[4,256,512]{2,1,0:T(8,128)(2,1)S(1)}, u32[]{:S(2)}) %copy-start) | copy-done | bytes 1048600
  49.6 4.0 %shard_map.56 = bf16[4,256,512]{2,1,0:T(8,128)(2,1)} custom-call(s32[4]{0:T(128)} %owner_ref.1, bf16[4,256,512]{2,1,0:T(8,128)(2,1)} %copy-done), custom_call_target="tpu_custom_call" | custom-call | tf_op jit(solution)/shard_map/pallas_call | solution.py:239
Async XLA Ops:
  0.0 1.6 %copy-start.1 = (bf16[1024,1024]{1,0:T(8,128)(2,1)S(1)}, bf16[1024,1024]{1,0:T(8,128)(2,1)}, u32[]{:S(2)}) copy-start(bf16[1024,1024]{1,0:T(8,128)(2,1)} %int_hbm.1) | copy-start | bytes 6291460
  1.6 1.0 %copy-start.2 = (bf16[256,1024]{1,0:T(8,128)(2,1)S(1)}, bf16[256,1024]{1,0:T(8,128)(2,1)}, u32[]{:S(2)}) copy-start(bf16[256,1024]{1,0:T(8,128)(2,1)} %amp_hbm.1) | copy-start | bytes 1572868
  2.6 0.7 %copy-start.3 = (s32[8,8]{1,0:T(8,128)S(1)}, s32[8,8]{1,0:T(8,128)}, u32[]{:S(2)}) copy-start(s32[8,8]{1,0:T(8,128)} %int_mask.1) | copy-start | bytes 772
  3.3 0.7 %copy-start.4 = (s32[2,8]{1,0:T(2,128)S(1)}, s32[2,8]{1,0:T(2,128)}, u32[]{:S(2)}) copy-start(s32[2,8]{1,0:T(2,128)} %amp_mask.1) | copy-start | bytes 196
  48.7 1.0 %copy-start = (bf16[4,256,512]{2,1,0:T(8,128)(2,1)}, bf16[4,256,512]{2,1,0:T(8,128)(2,1)S(1)}, u32[]{:S(2)}) copy-start(bf16[4,256,512]{2,1,0:T(8,128)(2,1)S(1)} %shard_map.55.block_ref) | copy-start | bytes 3145732

commit v2 on v1

--- a/solution.py
+++ b/solution.py
@@ -41,8 +41,8 @@
 
 
 def gather_kernel(
-    n, reps, amp_mask, int_mask, amp_hbm, int_hbm, out_ref,
-    blocks, ints, mine, sent, got,
+    n, reps, owner_hbm, amp_mask_hbm, int_mask_hbm, amp_hbm, int_hbm, out_ref,
+    owner, amp_mask, int_mask, blocks, ints, mine, sent, got,
     load_sem, up_send, up_recv, down_send, down_recv, x_send, x_recv,
 ):
     z = lax.axis_index("tile")
@@ -51,6 +51,13 @@
     part = rows // CHUNKS
     width = int_hbm.shape[1] // reps
 
+    loads = [
+        pltpu.make_async_copy(source, target, load_sem.at[2 + at])
+        for at, (source, target) in enumerate(
+            ((amp_mask_hbm, amp_mask), (int_mask_hbm, int_mask), (owner_hbm, owner)))
+    ]
+    for load in loads:
+        load.start()
     load_amp = pltpu.make_async_copy(amp_hbm, blocks.at[z], load_sem.at[0])
     load_int = pltpu.make_async_copy(int_hbm, ints, load_sem.at[1])
     load_amp.start()
@@ -109,8 +116,10 @@
         for k in range(1, reps):
             across(k, b, c).wait_recv()
             total = total + got[k - 1, b, span(c), :].astype(jnp.float32)
-        out_ref[b, span(c), :] = total.astype(jnp.bfloat16)
-
+        mine[b, span(c), :] = total.astype(jnp.bfloat16)
+
+    for load in loads:
+        load.wait()
     load_amp.wait()
     for c in range(CHUNKS):
         at = slice(c * part, (c + 1) * part)
@@ -188,6 +197,9 @@
         def _():
             finish(n - 1, c)
 
+    for step in range(out_ref.shape[0]):
+        out_ref[step] = mine[owner[step]]
+
     @pl.loop(0, n)
     def _(b):
         @pl.loop(0, CHUNKS)
@@ -202,10 +214,6 @@
             @pl.when((b >= z) & (z > 0))
             def _():
                 down(b, c).wait_send()
-
-
-def pick_kernel(owner_ref, block_ref, out_ref):
-    out_ref[...] = block_ref[...]
 
 
 def gathered(n, reps, amplitudes, amp_mask, integrals, int_mask, owner_map):
@@ -215,37 +223,30 @@
     steps = owner_map.shape[0]
     dma = pltpu.SemaphoreType.DMA
     bf16 = jnp.bfloat16
-    by_owner = pl.pallas_call(
+    return pl.pallas_call(
         functools.partial(gather_kernel, n, reps),
-        out_shape=jax.ShapeDtypeStruct((n, rows, width), bf16),
-        in_specs=[pl.BlockSpec(memory_space=pltpu.SMEM)] * 2 + [pl.BlockSpec(memory_space=pl.ANY)] * 2,
+        out_shape=jax.ShapeDtypeStruct((steps, rows, width), bf16),
+        in_specs=[pl.BlockSpec(memory_space=pl.ANY)] * 5,
         out_specs=pl.BlockSpec(memory_space=pltpu.VMEM),
         scratch_shapes=[
+            pltpu.SMEM(owner_map.shape, jnp.int32),
+            pltpu.SMEM(amp_mask.shape, jnp.int32),
+            pltpu.SMEM(int_mask.shape, jnp.int32),
             pltpu.VMEM((n, rows, depth), bf16),
             pltpu.VMEM((depth, wide), bf16),
             pltpu.VMEM((n, rows, width), bf16),
             pltpu.VMEM((reps - 1, n, rows, width), bf16),
             pltpu.VMEM((reps - 1, n, rows, width), bf16),
-            dma((2,)),
+            dma((5,)),
             dma((n, CHUNKS)), dma((n, CHUNKS)), dma((n, CHUNKS)), dma((n, CHUNKS)),
             dma((reps - 1, n, CHUNKS)), dma((reps - 1, n, CHUNKS)),
         ],
         compiler_params=pltpu.CompilerParams(
-            collective_id=0, has_side_effects=True, vmem_limit_bytes=40 * 1024 * 1024),
+            collective_id=0, has_side_effects=True, vmem_limit_bytes=62 * 1024 * 1024),
         cost_estimate=pl.CostEstimate(
             flops=2 * n * rows * depth * wide, bytes_accessed=2 * (rows * depth + depth * wide + n * rows * width),
             transcendentals=0),
-    )(amp_mask, int_mask, amplitudes, integrals)
-    return pl.pallas_call(
-        pick_kernel,
-        out_shape=jax.ShapeDtypeStruct((steps, rows, width), bf16),
-        grid_spec=pltpu.PrefetchScalarGridSpec(
-            num_scalar_prefetch=1,
-            grid=(steps,),
-            in_specs=[pl.BlockSpec((1, rows, width), lambda s, owner: (owner[s], 0, 0))],
-            out_specs=pl.BlockSpec((1, rows, width), lambda s, owner: (s, 0, 0)),
-        ),
-    )(owner_map, by_owner)
+    )(owner_map, amp_mask, int_mask, amplitudes, integrals)
 
 
 def solution(mesh):

time: 54 us -> 47.4 us (0.88)
  Pallas kernels: 48.7 us -> 45 us
  local copies, waits for them, and re-layouts: 4.95 us -> 2.26 us
    pallas_call x1 -> x0, Pallas kernels: 4.03 us -> none  [gathered(): pl.pallas_call(pick_kernel, out_shape=jax.ShapeDtypeStruct((steps, rows,...]
    unnamed x10 -> x1, local copies, waits for them, and re-layouts: 4.95 us -> 2.26 us
where the time goes in v2:
time: 47.4 us; the launch traced here: 47.2 us
  Pallas kernels  45 us (95%)
  local copies, waits for them, and re-layouts  2.26 us (5%)
    pallas_call x1, Pallas kernels, gathered(): pl.pallas_call(functools.partial(gather_kernel, n, reps), out_shape=jax.S...  45 us
    unnamed x1, local copies, waits for them, and re-layouts  2.26 us

profile of v2, /device:TPU:0, one launch (start us, length us, event | category | flops | bytes accessed | tf_op | source)
XLA Modules:
  0.0 47.2 jit_solution(17915210737430685018)
XLA Ops:
  0.0 45.0 %shard_map.55 = bf16[4,256,512]{2,1,0:T(8,128)(2,1)} custom-call(s32[4]{0:T(128)} %owner_hbm.1, s32[2,8]{1,0:T(2,128)} %amp_mask_hbm.1, s32[8,8]{1,0:T(8,128)} %int_mask_hbm.1, bf16[256,1024]{1,0:T(8,128)(2,1)} %amp_hbm.1, bf16[1024,1024]{1,0:T(8,128)(2,1)} %int_hbm.1), custom_call_target="tpu_custom_call" | custom-call | flops 2147483648 | bytes 3670016 | tf_op jit(solution)/shard_map/pallas_call | solution.py:226
  45.0 2.3 %copy.7 = bf16[4,256,512]{2,1,0:T(8,128)(2,1)} copy(bf16[4,256,512]{2,1,0:T(8,128)(2,1)} %shard_map.55) | data formatting | bytes 2097152

commit v3 on v2

--- a/solution.py
+++ b/solution.py
@@ -242,11 +242,12 @@
             dma((reps - 1, n, CHUNKS)), dma((reps - 1, n, CHUNKS)),
         ],
         compiler_params=pltpu.CompilerParams(
-            collective_id=0, has_side_effects=True, vmem_limit_bytes=62 * 1024 * 1024),
+            collective_id=0, has_side_effects=True, vmem_limit_bytes=24 * 1024 * 1024),
         cost_estimate=pl.CostEstimate(
             flops=2 * n * rows * depth * wide, bytes_accessed=2 * (rows * depth + depth * wide + n * rows * width),
             transcendentals=0),
-    )(owner_map, amp_mask, int_mask, amplitudes, integrals)
+    )(*(pltpu.with_memory_space_constraint(each, pltpu.HBM)
+        for each in (owner_map, amp_mask, int_mask, amplitudes, integrals)))
 
 
 def solution(mesh):

time: 47.4 us -> 45.1 us (0.951)
  local copies, waits for them, and re-layouts: 2.26 us -> 0.97 us
  Pallas kernels: 45 us -> 44 us
    unnamed x1, local copies, waits for them, and re-layouts: 2.26 us -> 0.97 us
    pallas_call x1, Pallas kernels: 45 us -> 44 us  [gathered(): pl.pallas_call(functools.partial(gather_kernel, n, reps), out_shape=jax.S...]
where the time goes in v3:
time: 45.1 us; the launch traced here: 44.9 us
  Pallas kernels  44 us (98%)
  local copies, waits for them, and re-layouts  0.97 us (2%)
    pallas_call x1, Pallas kernels, gathered(): pl.pallas_call(functools.partial(gather_kernel, n, reps), out_shape=jax.S...  44 us
    unnamed x1, local copies, waits for them, and re-layouts  0.97 us

profile of v3, /device:TPU:0, one launch (start us, length us, event | category | flops | bytes accessed | tf_op | source)
XLA Modules:
  0.0 44.9 jit_solution(8806194008826446093)
XLA Ops:
  0.0 44.0 %shard_map.55 = bf16[4,256,512]{2,1,0:T(8,128)(2,1)S(1)} custom-call(s32[4]{0:T(128)} %owner_hbm.1, s32[2,8]{1,0:T(2,128)} %amp_mask_hbm.1, s32[8,8]{1,0:T(8,128)} %int_mask_hbm.1, bf16[256,1024]{1,0:T(8,128)(2,1)} %amp_hbm.1, bf16[1024,1024]{1,0:T(8,128)(2,1)} %int_hbm.1), custom_call_target="tpu_custom_call" | custom-call | flops 2147483648 | bytes 3670016 | tf_op jit(solution)/shard_map/pallas_call | solution.py:226
  44.0 1.0 %copy.7 = bf16[4,256,512]{2,1,0:T(8,128)(2,1)} copy(bf16[4,256,512]{2,1,0:T(8,128)(2,1)S(1)} %shard_map.55) | data formatting | bytes 2097152

commit v4 on v3

--- a/solution.py
+++ b/solution.py
@@ -42,14 +42,22 @@
 
 def gather_kernel(
     n, reps, owner_hbm, amp_mask_hbm, int_mask_hbm, amp_hbm, int_hbm, out_ref,
-    owner, amp_mask, int_mask, blocks, ints, mine, sent, got,
+    owner, amp_mask, int_mask, blocks, ints, mine, sent, got, end_ints, help_mine, help_sent, help_got,
     load_sem, up_send, up_recv, down_send, down_recv, x_send, x_recv,
+    int_send, int_recv, y_send, y_recv, sub_send, sub_recv, help_send, help_recv, back_send, back_recv,
 ):
     z = lax.axis_index("tile")
     x = lax.axis_index("rep")
     rows, depth = amp_hbm.shape
     part = rows // CHUNKS
     width = int_hbm.shape[1] // reps
+    group, sub = lax.axis_index("groups"), lax.axis_index("sub")
+    is_end = (z == 0) | (z == n - 1)
+    is_helper = (z == 1) | (z == n - 2)
+    helper = jnp.where(z == 0, 1, n - 2)
+    end = jnp.where(z == 1, 0, n - 1)
+    quarter = depth // 4
+    slab = quarter // CHUNKS
 
     loads = [
         pltpu.make_async_copy(source, target, load_sem.at[2 + at])
@@ -75,7 +83,13 @@
 
     for k in range(1, reps):
         pl.semaphore_signal(barrier, inc=1, device_id={"rep": lax.rem(x + k, reps)}, device_id_type=MESH)
-    pl.semaphore_wait(barrier, jnp.where(z > 0, 1, 0) + jnp.where(z < n - 1, 1, 0) + (reps - 1))
+
+    @pl.when(is_helper)
+    def _():
+        pl.semaphore_signal(barrier, inc=1, device_id={"groups": 1 - group}, device_id_type=MESH)
+        pl.semaphore_signal(barrier, inc=1, device_id={"sub": 1 - sub}, device_id_type=MESH)
+
+    pl.semaphore_wait(barrier, jnp.where(is_helper, 2, 0) + jnp.where(z > 0, 1, 0) + jnp.where(z < n - 1, 1, 0) + (reps - 1))
 
     def span(c):
         return pl.ds(pl.multiple_of(c * part, part), part)
@@ -97,6 +111,69 @@
             src_ref=sent.at[k - 1, b, span(c)], dst_ref=got.at[k - 1, b, span(c)],
             send_sem=x_send.at[k - 1, b, c], recv_sem=x_recv.at[k - 1, b, c],
             device_id={"rep": lax.rem(x + k, reps)}, device_id_type=MESH)
+
+    def slab_of(g, u, c):
+        return pl.ds(pl.multiple_of((g * 2 + u) * quarter + c * slab, slab), slab)
+
+    def to_helper(c):
+        return pltpu.make_async_remote_copy(
+            src_ref=ints.at[slab_of(group, sub, c)], dst_ref=end_ints.at[slab_of(group, sub, c)],
+            send_sem=int_send.at[c], recv_sem=int_recv.at[c], device_id={"tile": helper}, device_id_type=MESH)
+
+    def from_end(c):
+        piece = end_ints.at[slab_of(group, sub, c)]
+        return pltpu.make_async_remote_copy(
+            src_ref=piece, dst_ref=piece,
+            send_sem=int_send.at[c], recv_sem=int_recv.at[c], device_id={"tile": end}, device_id_type=MESH)
+
+    def over_y(g, c):
+        piece = end_ints.at[slab_of(g, sub, c)]
+        return pltpu.make_async_remote_copy(
+            src_ref=piece, dst_ref=piece, send_sem=y_send.at[c], recv_sem=y_recv.at[c],
+            device_id={"groups": 1 - group}, device_id_type=MESH)
+
+    def over_sub(k, u, c):
+        piece = end_ints.at[slab_of(group if k == 0 else 1 - group, u, c)]
+        return pltpu.make_async_remote_copy(
+            src_ref=piece, dst_ref=piece, send_sem=sub_send.at[k, c], recv_sem=sub_recv.at[k, c],
+            device_id={"sub": 1 - sub}, device_id_type=MESH)
+
+    def help_across(c):
+        return pltpu.make_async_remote_copy(
+            src_ref=help_sent.at[span(c)], dst_ref=help_got.at[span(c)],
+            send_sem=help_send.at[c], recv_sem=help_recv.at[c],
+            device_id={"rep": 1 - x}, device_id_type=MESH)
+
+    def back(b, to, c):
+        return pltpu.make_async_remote_copy(
+            src_ref=help_mine.at[span(c)], dst_ref=mine.at[b, span(c)],
+            send_sem=back_send.at[c], recv_sem=back_recv.at[c],
+            device_id={"tile": to}, device_id_type=MESH)
+
+    def pass_on(c):
+        over_y(1 - group, c).wait_recv()
+        over_sub(1, sub, c).start()
+
+    def help_compute(c):
+        help_sent[span(c), :] = jnp.dot(
+            blocks[z, span(c), :], end_ints[:, columns(1 - x)],
+            preferred_element_type=jnp.float32).astype(jnp.bfloat16)
+        help_across(c).start()
+        help_mine[span(c), :] = jnp.dot(
+            blocks[z, span(c), :], end_ints[:, columns(x)],
+            preferred_element_type=jnp.float32).astype(jnp.bfloat16)
+
+    def help_finish(c):
+        help_across(c).wait_recv()
+        total = help_mine[span(c), :].astype(jnp.float32) + help_got[span(c), :].astype(jnp.float32)
+        help_mine[span(c), :] = total.astype(jnp.bfloat16)
+        back(z, end, c).start()
+
+    def mask_ints(i):
+        for j in range(int_hbm.shape[1] // TILE):
+            at = pl.ds(pl.multiple_of(i * TILE, TILE), TILE)
+            here = slice(j * TILE, (j + 1) * TILE)
+            ints[at, here] = ints[at, here] * tile_scale(int_mask, i, j, (TILE, TILE))
 
     def columns(r):
         return pl.ds(pl.multiple_of(r * width, width), width)
@@ -120,6 +197,21 @@
 
     for load in loads:
         load.wait()
+
+    tall = depth // TILE
+    first = (group * 2 + sub) * (quarter // TILE)
+
+    @pl.when(is_end)
+    def _():
+        load_int.wait()
+
+        @pl.loop(0, quarter // TILE)
+        def _(i):
+            mask_ints(first + i)
+
+        for c in range(CHUNKS):
+            to_helper(c).start()
+
     load_amp.wait()
     for c in range(CHUNKS):
         at = slice(c * part, (c + 1) * part)
@@ -128,74 +220,124 @@
             scale = tile_scale(amp_mask, c * part // TILE, j, (part, TILE))
             blocks[z, at, here] = blocks[z, at, here] * scale
 
-        @pl.when(z < n - 1)
+        @pl.when(z < n - 2)
         def _():
             up(z, c).start()
 
-        @pl.when(z > 0)
+        @pl.when(z > 1)
         def _():
             down(z, c).start()
 
-    load_int.wait()
-    for j in range(int_hbm.shape[1] // TILE):
-        here = slice(j * TILE, (j + 1) * TILE)
-
-        @pl.loop(0, depth // TILE)
+    @pl.when(jnp.logical_not(is_end))
+    def _():
+        load_int.wait()
+
+        @pl.loop(0, quarter // TILE)
         def _(i):
-            at = pl.ds(pl.multiple_of(i * TILE, TILE), TILE)
-            ints[at, here] = ints[at, here] * tile_scale(int_mask, i, j, (TILE, TILE))
+            mask_ints(first + i)
+
+    @pl.loop(quarter // TILE, tall)
+    def _(i):
+        mask_ints(lax.rem(first + i, tall))
 
     @pl.loop(0, CHUNKS)
     def _(c):
         compute(z, c)
 
+    w = n - 1 - z
+
+    def comes(far, d):
+        near = (d == 1) & (far > 1) & (far < n - 1)
+        return near | ((d > 1) & (far - d >= 0)) | ((d == 2) & (far == 1))
+
+    def lower(d):
+        return jnp.maximum(z - d, 0)
+
+    def upper(d):
+        return n - 1 - jnp.maximum(w - d, 0)
+
+    def finish_all(d, c):
+        @pl.when(d == 0)
+        def _():
+            finish(z, c)
+
+        @pl.when(comes(z, d))
+        def _():
+            finish(lower(d), c)
+
+        @pl.when(comes(w, d))
+        def _():
+            finish(upper(d), c)
+
     @pl.loop(1, n)
     def _(d):
-        lower, upper = z - d, z + d
-
         @pl.loop(0, CHUNKS)
         def _(c):
-            @pl.when(lower >= 0)
-            def _():
-                up(lower, c).wait_recv()
+            @pl.when(is_helper & (d == 1))
+            def _():
+                from_end(c).wait_recv()
+                over_y(group, c).start()
+                over_sub(0, sub, c).start()
+
+            @pl.when(comes(z, d))
+            def _():
+                up(lower(d), c).wait_recv()
 
                 @pl.when(z < n - 1)
                 def _():
-                    up(lower, c).start()
-
-            @pl.when(upper < n)
-            def _():
-                down(upper, c).wait_recv()
+                    up(lower(d), c).start()
+
+            @pl.when(comes(w, d))
+            def _():
+                down(upper(d), c).wait_recv()
 
                 @pl.when(z > 0)
                 def _():
-                    down(upper, c).start()
-
-            @pl.when(lower >= 0)
-            def _():
-                compute(lower, c)
-
-            @pl.when(upper < n)
-            def _():
-                compute(upper, c)
-
-            @pl.when(lower + 1 >= 0)
-            def _():
-                finish(lower + 1, c)
-
-            @pl.when((upper - 1 < n) & (d > 1))
-            def _():
-                finish(upper - 1, c)
+                    down(upper(d), c).start()
+
+            @pl.when(is_helper & (d == 1) & (c > 0))
+            def _():
+                pass_on(c - 1)
+
+            @pl.when(comes(z, d))
+            def _():
+                compute(lower(d), c)
+
+            @pl.when(comes(w, d))
+            def _():
+                compute(upper(d), c)
+
+            @pl.when(is_helper & (d == 2))
+            def _():
+                @pl.when(c == 0)
+                def _():
+                    for piece in range(CHUNKS):
+                        over_sub(0, 1 - sub, piece).wait_recv()
+                        over_sub(1, 1 - sub, piece).wait_recv()
+
+                help_compute(c)
+
+                @pl.when(c > 0)
+                def _():
+                    help_finish(c - 1)
+
+            finish_all(d - 1, c)
+
+        @pl.when(is_helper & (d == 1))
+        def _():
+            pass_on(CHUNKS - 1)
+
+        @pl.when(is_helper & (d == 2))
+        def _():
+            help_finish(CHUNKS - 1)
 
     @pl.loop(0, CHUNKS)
     def _(c):
-        @pl.when(z == n - 1)
-        def _():
-            finish(0, c)
-
-        @pl.when(z == 0)
-        def _():
-            finish(n - 1, c)
+        finish_all(n - 1, c)
+
+        @pl.when(is_end)
+        def _():
+            back(helper, helper, c).wait_recv()
 
     for step in range(out_ref.shape[0]):
         out_ref[step] = mine[owner[step]]
@@ -204,16 +346,32 @@
     def _(b):
         @pl.loop(0, CHUNKS)
         def _(c):
-            for k in range(1, reps):
-                across(k, b, c).wait_send()
-
-            @pl.when((b <= z) & (z < n - 1))
+            @pl.when(jnp.logical_not(is_end & (b == helper)))
+            def _():
+                for k in range(1, reps):
+                    across(k, b, c).wait_send()
+
+            @pl.when((b <= z) & (z < n - 1) & (b != n - 2))
             def _():
                 up(b, c).wait_send()
 
-            @pl.when((b >= z) & (z > 0))
+            @pl.when((b >= z) & (z > 0) & (b != 1))
             def _():
                 down(b, c).wait_send()
+
+    @pl.loop(0, CHUNKS)
+    def _(c):
+        @pl.when(is_end)
+        def _():
+            to_helper(c).wait_send()
+
+        @pl.when(is_helper)
+        def _():
+            over_y(group, c).wait_send()
+            over_sub(0, sub, c).wait_send()
+            over_sub(1, sub, c).wait_send()
+            help_across(c).wait_send()
+            back(z, end, c).wait_send()
 
 
 def gathered(n, reps, amplitudes, amp_mask, integrals, int_mask, owner_map):
@@ -237,9 +395,16 @@
             pltpu.VMEM((n, rows, width), bf16),
             pltpu.VMEM((reps - 1, n, rows, width), bf16),
             pltpu.VMEM((reps - 1, n, rows, width), bf16),
+            pltpu.VMEM((depth, wide), bf16),
+            pltpu.VMEM((rows, width), bf16),
+            pltpu.VMEM((rows, width), bf16),
+            pltpu.VMEM((rows, width), bf16),
             dma((5,)),
             dma((n, CHUNKS)), dma((n, CHUNKS)), dma((n, CHUNKS)), dma((n, CHUNKS)),
             dma((reps - 1, n, CHUNKS)), dma((reps - 1, n, CHUNKS)),
+            dma((CHUNKS,)), dma((CHUNKS,)), dma((CHUNKS,)), dma((CHUNKS,)),
+            dma((2, CHUNKS)), dma((2, CHUNKS)),
+            dma((CHUNKS,)), dma((CHUNKS,)), dma((CHUNKS,)), dma((CHUNKS,)),
         ],
         compiler_params=pltpu.CompilerParams(
             collective_id=0, has_side_effects=True, vmem_limit_bytes=24 * 1024 * 1024),
@@ -252,9 +417,10 @@
 
 def solution(mesh):
     n, reps = mesh.shape["tile"], mesh.shape["rep"]
+    pairs = mesh.shape["groups"] == mesh.shape["sub"] == reps == 2
 
     def shards(amplitudes, amp_mask, integrals, int_mask, owner_map):
-        if n > owner_map.shape[0]:
+        if n > owner_map.shape[0] or n != 4 or not pairs:
             return stepwise(amplitudes, amp_mask, integrals, int_mask, owner_map)
         return gathered(n, reps, amplitudes, amp_mask, integrals, int_mask, owner_map)
 

time: 45.1 us -> 70.6 us (1.57)
  Pallas kernels: 44 us -> 69.5 us
    pallas_call x1, Pallas kernels: 44 us -> 69.5 us  [gathered(): pl.pallas_call(functools.partial(gather_kernel, n, reps), out_shape=jax.S...]
where the time goes in v4:
time: 70.6 us; the launch traced here: 70.5 us
  Pallas kernels  69.5 us (98%)
  local copies, waits for them, and re-layouts  0.97 us (1%)
    pallas_call x1, Pallas kernels, gathered(): pl.pallas_call(functools.partial(gather_kernel, n, reps), out_shape=jax.S...  69.5 us

profile of v4, /device:TPU:0, one launch (start us, length us, event | category | flops | bytes accessed | tf_op | source)
XLA Modules:
  0.0 70.5 jit_solution(2531791491314341193)
XLA Ops:
  0.0 69.5 %shard_map.55 = bf16[4,256,512]{2,1,0:T(8,128)(2,1)S(1)} custom-call(s32[4]{0:T(128)} %owner_hbm.1, s32[2,8]{1,0:T(2,128)} %amp_mask_hbm.1, s32[8,8]{1,0:T(8,128)} %int_mask_hbm.1, bf16[256,1024]{1,0:T(8,128)(2,1)} %amp_hbm.1, bf16[1024,1024]{1,0:T(8,128)(2,1)} %int_hbm.1), custom_call_target="tpu_custom_call" | custom-call | flops 2147483648 | bytes 3670016 | tf_op jit(solution)/shard_map/pallas_call | solution.py:384
  69.5 1.0 %copy.7 = bf16[4,256,512]{2,1,0:T(8,128)(2,1)} copy(bf16[4,256,512]{2,1,0:T(8,128)(2,1)S(1)} %shard_map.55) | data formatting | bytes 2097152

commit v5 on v4

--- a/solution.py
+++ b/solution.py
@@ -201,17 +201,6 @@
     tall = depth // TILE
     first = (group * 2 + sub) * (quarter // TILE)
 
-    @pl.when(is_end)
-    def _():
-        load_int.wait()
-
-        @pl.loop(0, quarter // TILE)
-        def _(i):
-            mask_ints(first + i)
-
-        for c in range(CHUNKS):
-            to_helper(c).start()
-
     load_amp.wait()
     for c in range(CHUNKS):
         at = slice(c * part, (c + 1) * part)
@@ -228,6 +217,17 @@
         def _():
             down(z, c).start()
 
+    @pl.when(is_end)
+    def _():
+        load_int.wait()
+
+        @pl.loop(0, quarter // TILE)
+        def _(i):
+            mask_ints(first + i)
+
+        for c in range(CHUNKS):
+            to_helper(c).start()
+
     @pl.when(jnp.logical_not(is_end))
     def _():
         load_int.wait()
@@ -247,8 +247,7 @@
     w = n - 1 - z
 
     def comes(far, d):
-        near = (d == 1) & (far > 1) & (far < n - 1)
-        return near | ((d > 1) & (far - d >= 0)) | ((d == 2) & (far == 1))
+        return (far - d >= 0) & ((d > 1) | ((d == 1) & (far < n - 1)))
 
     def lower(d):
         return jnp.maximum(z - d, 0)
@@ -273,41 +272,41 @@
     def _(d):
         @pl.loop(0, CHUNKS)
         def _(c):
-            @pl.when(is_helper & (d == 1))
+            @pl.when(comes(z, d))
+            def _():
+                up(lower(d), c).wait_recv()
+
+                @pl.when(z < n - 1)
+                def _():
+                    up(lower(d), c).start()
+
+            @pl.when(comes(w, d))
+            def _():
+                down(upper(d), c).wait_recv()
+
+                @pl.when(z > 0)
+                def _():
+                    down(upper(d), c).start()
+
+            @pl.when(is_helper & (d == 2))
             def _():
                 from_end(c).wait_recv()
                 over_y(group, c).start()
                 over_sub(0, sub, c).start()
 
+            @pl.when(is_helper & (d == 2) & (c > 0))
+            def _():
+                pass_on(c - 1)
+
             @pl.when(comes(z, d))
             def _():
-                up(lower(d), c).wait_recv()
-
-                @pl.when(z < n - 1)
-                def _():
-                    up(lower(d), c).start()
+                compute(lower(d), c)
 
             @pl.when(comes(w, d))
             def _():
-                down(upper(d), c).wait_recv()
-
-                @pl.when(z > 0)
-                def _():
-                    down(upper(d), c).start()
-
-            @pl.when(is_helper & (d == 1) & (c > 0))
-            def _():
-                pass_on(c - 1)
-
-            @pl.when(comes(z, d))
-            def _():
-                compute(lower(d), c)
-
-            @pl.when(comes(w, d))
-            def _():
                 compute(upper(d), c)
 
-            @pl.when(is_helper & (d == 2))
+            @pl.when(is_helper & (d == 3))
             def _():
                 @pl.when(c == 0)
                 def _():
@@ -323,11 +322,11 @@
 
             finish_all(d - 1, c)
 
-        @pl.when(is_helper & (d == 1))
+        @pl.when(is_helper & (d == 2))
         def _():
             pass_on(CHUNKS - 1)
 
-        @pl.when(is_helper & (d == 2))
+        @pl.when(is_helper & (d == 3))
         def _():
             help_finish(CHUNKS - 1)
 

time: 70.6 us -> 49.4 us (0.70)
  Pallas kernels: 69.5 us -> 48.3 us
    pallas_call x1, Pallas kernels: 69.5 us -> 48.3 us  [gathered(): pl.pallas_call(functools.partial(gather_kernel, n, reps), out_shape=jax.S...]
where the time goes in v5:
time: 49.4 us; the launch traced here: 49.2 us
  Pallas kernels  48.3 us (98%)
  local copies, waits for them, and re-layouts  0.97 us (2%)
    pallas_call x1, Pallas kernels, gathered(): pl.pallas_call(functools.partial(gather_kernel, n, reps), out_shape=jax.S...  48.3 us

profile of v5, /device:TPU:0, one launch (start us, length us, event | category | flops | bytes accessed | tf_op | source)
XLA Modules:
  0.0 49.2 jit_solution(10515009333173265893)
XLA Ops:
  0.0 48.3 %shard_map.55 = bf16[4,256,512]{2,1,0:T(8,128)(2,1)S(1)} custom-call(s32[4]{0:T(128)} %owner_hbm.1, s32[2,8]{1,0:T(2,128)} %amp_mask_hbm.1, s32[8,8]{1,0:T(8,128)} %int_mask_hbm.1, bf16[256,1024]{1,0:T(8,128)(2,1)} %amp_hbm.1, bf16[1024,1024]{1,0:T(8,128)(2,1)} %int_hbm.1), custom_call_target="tpu_custom_call" | custom-call | flops 2147483648 | bytes 3670016 | tf_op jit(solution)/shard_map/pallas_call | solution.py:383
  48.3 1.0 %copy.7 = bf16[4,256,512]{2,1,0:T(8,128)(2,1)} copy(bf16[4,256,512]{2,1,0:T(8,128)(2,1)S(1)} %shard_map.55) | data formatting | bytes 2097152

commit v6 on v3

--- a/solution.py
+++ b/solution.py
@@ -56,13 +56,11 @@
         for at, (source, target) in enumerate(
             ((amp_mask_hbm, amp_mask), (int_mask_hbm, int_mask), (owner_hbm, owner)))
     ]
-    for load in loads:
-        load.start()
     load_amp = pltpu.make_async_copy(amp_hbm, blocks.at[z], load_sem.at[0])
     load_int = pltpu.make_async_copy(int_hbm, ints, load_sem.at[1])
+
     load_amp.start()
-    load_int.start()
-
+    loads[0].start()
     barrier = pltpu.get_barrier_semaphore()
 
     @pl.when(z > 0)
@@ -118,9 +116,11 @@
             total = total + got[k - 1, b, span(c), :].astype(jnp.float32)
         mine[b, span(c), :] = total.astype(jnp.bfloat16)
 
-    for load in loads:
-        load.wait()
+    loads[0].wait()
     load_amp.wait()
+    load_int.start()
+    for load in loads[1:]:
+        load.start()
     for c in range(CHUNKS):
         at = slice(c * part, (c + 1) * part)
         for j in range(depth // TILE):
@@ -137,6 +137,8 @@
             down(z, c).start()
 
     load_int.wait()
+    for load in loads[1:]:
+        load.wait()
     for j in range(int_hbm.shape[1] // TILE):
         here = slice(j * TILE, (j + 1) * TILE)
 

time: 45.1 us -> 45.1 us (level)
  no operation moved by 1% of the time
where the time goes in v6:
time: 45.1 us; the launch traced here: 44.9 us
  Pallas kernels  43.9 us (97%)
  local copies, waits for them, and re-layouts  0.97 us (2%)
    pallas_call x1, Pallas kernels, gathered(): pl.pallas_call(functools.partial(gather_kernel, n, reps), out_shape=jax.S...  43.9 us
    unnamed x1, local copies, waits for them, and re-layouts  0.97 us

profile of v6, /device:TPU:0, one launch (start us, length us, event | category | flops | bytes accessed | tf_op | source)
XLA Modules:
  0.0 44.9 jit_solution(13815228309286694982)
XLA Ops:
  0.0 43.9 %shard_map.55 = bf16[4,256,512]{2,1,0:T(8,128)(2,1)S(1)} custom-call(s32[4]{0:T(128)} %owner_hbm.1, s32[2,8]{1,0:T(2,128)} %amp_mask_hbm.1, s32[8,8]{1,0:T(8,128)} %int_mask_hbm.1, bf16[256,1024]{1,0:T(8,128)(2,1)} %amp_hbm.1, bf16[1024,1024]{1,0:T(8,128)(2,1)} %int_hbm.1), custom_call_target="tpu_custom_call" | custom-call | flops 2147483648 | bytes 3670016 | tf_op jit(solution)/shard_map/pallas_call | solution.py:228
  44.0 1.0 %copy.7 = bf16[4,256,512]{2,1,0:T(8,128)(2,1)} copy(bf16[4,256,512]{2,1,0:T(8,128)(2,1)S(1)} %shard_map.55) | data formatting | bytes 2097152
